TPU v7x, 256 devices: a whole 4x4x8 slice. The times are simulated.
256 devices in a mesh: row: 16 (over z_hi, y, core), col: 16 (over x, z_lo).
Axes of the slice: x: 4, y: 4, z: 8 (z_hi: 2, z_lo: 4; z = z_hi * 4 + z_lo), core: 2. Of those that a mesh axis runs over, the one named last changes fastest.
Arguments:
- vectors: float32 [32, 1, 16, 16, 256], P(None, None, 'row', 'col'), may hold values from -6 to 6
- tiles: bfloat16 [16, 16, 80, 256, 256], P('row', 'col'), may hold values from -0.0390625 to 0.0390625
- pattern: int32 [16, 16, 80, 2], P('row', 'col'), may hold values from -1 to 255, as said below
Outputs:
- filtered: float32 [32, 1, 16, 16, 256], P(None, None, 'row', 'col')
Inputs may be any that keep to these rules, and one draw needn't show every extreme that they name: pattern[r, c, s] = (i, j) with i <= j, (i // 16) % 16 == r and j % 16 == c, or (-1, -1) for an empty slot. Live slots come first in each grid position's list, and some grid position has all 80 slots live. A pair may occur more than once; its tiles then add.
All inputs are finite; a program needn't handle non-finite values.
Results may differ from a plain program's by a relative error of at most 0.0085.
Values may be sent and summed in bfloat16 or wider, within the bound.
A program may use at most 64 MiB of HBM per device.

v0:
```python
import jax
import jax.numpy as jnp
from jax import lax
from jax.sharding import PartitionSpec as P

DEG = 5


CENTER = 0.5
HALF_WIDTH = 3.0


def per_device(vectors, tiles, pattern):
    rows_count = lax.axis_size("row")
    cols_count = lax.axis_size("col")
    vec_count = vectors.shape[0]
    blk_count = vectors.shape[1]
    tile_width = vectors.shape[4]
    present = jnp.transpose(vectors.reshape(vec_count, blk_count, tile_width), (1, 0, 2))
    tile_set = tiles[0, 0]
    slot_pairs = pattern[0, 0]
    live_slots = slot_pairs[:, 0] >= 0
    block_row = jnp.where(live_slots, slot_pairs[:, 0], 0)
    block_col = jnp.where(live_slots, slot_pairs[:, 1], 0)
    grid_size = rows_count * cols_count
    forward_index = block_row % cols_count * blk_count + block_row // grid_size
    mirror_index = block_col // cols_count % rows_count * blk_count + block_col // grid_size
    weight_mask = live_slots.astype(jnp.float32)[:, None, None]
    previous = present
    for term_index in range(DEG):
        rounded = present.astype(jnp.bfloat16)
        col_pieces = lax.all_gather(rounded, "row", axis=0, tiled=True)
        row_pieces = lax.all_gather(rounded, "col", axis=0, tiled=True)
        col_inputs = jnp.take(col_pieces, mirror_index, axis=0)
        row_inputs = jnp.take(row_pieces, forward_index, axis=0)
        forward_terms = (
            jnp.einsum("svb,sab->sva", col_inputs, tile_set, preferred_element_type=jnp.float32)
            * weight_mask
        )
        mirror_terms = (
            jnp.einsum("sva,sab->svb", row_inputs, tile_set, preferred_element_type=jnp.float32)
            * weight_mask
        )
        forward_part = (
            jnp.zeros((cols_count * blk_count, vec_count, tile_width), jnp.float32)
            .at[forward_index]
            .add(forward_terms)
        )
        mirror_part = (
            jnp.zeros((rows_count * blk_count, vec_count, tile_width), jnp.float32)
            .at[mirror_index]
            .add(mirror_terms)
        )
        forward_total = lax.psum_scatter(forward_part, "col", scatter_dimension=0, tiled=True)
        mirror_total = lax.psum_scatter(mirror_part, "row", scatter_dimension=0, tiled=True)
        product = forward_total + mirror_total
        scaled = (product - CENTER * present) / HALF_WIDTH
        if term_index == 0:
            following = scaled
        else:
            following = 2.0 * scaled - previous
        previous, present = (present, following)
    return jnp.transpose(present, (1, 0, 2)).reshape(vec_count, blk_count, 1, 1, tile_width)


def solution(mesh):
    placed = (
        P(None, None, "row", "col", None),
        P("row", "col", None, None, None),
        P("row", "col", None, None),
    )
    return jax.shard_map(
        per_device,
        mesh=mesh,
        in_specs=placed,
        out_specs=P(None, None, "row", "col", None),
        check_vma=False,
    )
```

profile of v0, /device:TPU:1, one launch (start us, length us, event | category | flops | bytes accessed | tf_op | source)
XLA Modules:
  0.0 1078.2 jit_solution(2937870177157619891)
XLA Ops:
  8.9 39.2 %all_gather.31 = bf16[16,32,256]{2,1,0:T(8,128)(2,1)S(1)} all-gather(bf16[1,32,256]{2,1,0:T(8,128)(2,1)S(1)} %bitcast.72), channel_id=1, replica_groups=mesh['row'=16,'col'=16] {'col'}, dimensions={0}, use_global_device_ids=true | all-gather | bytes 278528 | tf_op jit(solution)/shard_map/all_gather | solution.py:33
  49.9 6.3 fusion.23
  56.3 4.5 scatter_fusion.1
  61.7 39.5 %all_gather.30 = bf16[16,32,256]{2,1,0:T(8,128)(2,1)S(1)} all-gather(bf16[1,32,256]{2,1,0:T(8,128)(2,1)S(1)} %bitcast.73), channel_id=1, replica_groups=mesh['row'=16,'col'=16] {'row'}, dimensions={0}, use_global_device_ids=true | all-gather | bytes 278528 | tf_op jit(solution)/shard_map/all_gather | solution.py:32
  103.0 7.6 fusion.20
  116.1 26.0 %reduce-scatter.13.cloned.1.call-done = f32[1,32,256]{2,1,0:T(8,128)} async-done(((f32[16,32,256]{2,1,0:T(8,128)}), f32[1,32,256]{2,1,0:T(8,128)}) %reduce-scatter.13.cloned.1.call-update) | async-done | bytes 32784 | tf_op jit(solution)/shard_map/reduce_scatter | solution.py:55
  142.1 74.4 %reduce-scatter.11.cloned.1.call-done = f32[1,32,256]{2,1,0:T(8,128)} async-done(((f32[16,32,256]{2,1,0:T(8,128)}), f32[1,32,256]{2,1,0:T(8,128)}) %reduce-scatter.11.cloned.1.call-update) | async-done | bytes 32784 | tf_op jit(solution)/shard_map/reduce_scatter | solution.py:54
  217.2 33.1 %all_gather.33 = bf16[16,32,256]{2,1,0:T(8,128)(2,1)S(1)} all-gather(bf16[1,32,256]{2,1,0:T(8,128)(2,1)S(1)} %get-tuple-element.10), channel_id=1, replica_groups=mesh['row'=16,'col'=16] {'col'}, dimensions={0}, use_global_device_ids=true | all-gather | bytes 278528 | tf_op jit(solution)/shard_map/all_gather | solution.py:33
  252.2 6.3 fusion.29
  258.6 4.5 scatter_fusion.3
  264.0 50.6 %all_gather.32 = bf16[16,32,256]{2,1,0:T(8,128)(2,1)S(1)} all-gather(bf16[1,32,256]{2,1,0:T(8,128)(2,1)S(1)} %get-tuple-element.10), channel_id=1, replica_groups=mesh['row'=16,'col'=16] {'row'}, dimensions={0}, use_global_device_ids=true | all-gather | bytes 278528 | tf_op jit(solution)/shard_map/all_gather | solution.py:32
  316.4 7.6 fusion.26
  329.5 25.9 %reduce-scatter.17.cloned.1.call-done = f32[1,32,256]{2,1,0:T(8,128)} async-done(((f32[16,32,256]{2,1,0:T(8,128)}), f32[1,32,256]{2,1,0:T(8,128)}) %reduce-scatter.17.cloned.1.call-update) | async-done | bytes 32784 | tf_op jit(solution)/shard_map/reduce_scatter | solution.py:55
  355.4 73.6 %reduce-scatter.15.cloned.1.call-done = f32[1,32,256]{2,1,0:T(8,128)} async-done(((f32[16,32,256]{2,1,0:T(8,128)}), f32[1,32,256]{2,1,0:T(8,128)}) %reduce-scatter.15.cloned.1.call-update) | async-done | bytes 32784 | tf_op jit(solution)/shard_map/reduce_scatter | solution.py:54
  429.8 33.9 %all_gather.35 = bf16[16,32,256]{2,1,0:T(8,128)(2,1)S(1)} all-gather(bf16[1,32,256]{2,1,0:T(8,128)(2,1)S(1)} %get-tuple-element.8), channel_id=1, replica_groups=mesh['row'=16,'col'=16] {'col'}, dimensions={0}, use_global_device_ids=true | all-gather | bytes 278528 | tf_op jit(solution)/shard_map/all_gather | solution.py:33
  465.5 6.3 fusion.35
  477.4 50.5 %all_gather.34 = bf16[16,32,256]{2,1,0:T(8,128)(2,1)S(1)} all-gather(bf16[1,32,256]{2,1,0:T(8,128)(2,1)S(1)} %get-tuple-element.8), channel_id=1, replica_groups=mesh['row'=16,'col'=16] {'row'}, dimensions={0}, use_global_device_ids=true | all-gather | bytes 278528 | tf_op jit(solution)/shard_map/all_gather | solution.py:32
  529.7 7.6 fusion.32
  542.7 26.1 %reduce-scatter.21.cloned.1.call-done = f32[1,32,256]{2,1,0:T(8,128)} async-done(((f32[16,32,256]{2,1,0:T(8,128)}), f32[1,32,256]{2,1,0:T(8,128)}) %reduce-scatter.21.cloned.1.call-update) | async-done | bytes 32784 | tf_op jit(solution)/shard_map/reduce_scatter | solution.py:55
  568.9 74.2 %reduce-scatter.19.cloned.1.call-done = f32[1,32,256]{2,1,0:T(8,128)} async-done(((f32[16,32,256]{2,1,0:T(8,128)}), f32[1,32,256]{2,1,0:T(8,128)}) %reduce-scatter.19.cloned.1.call-update) | async-done | bytes 32784 | tf_op jit(solution)/shard_map/reduce_scatter | solution.py:54
  643.9 33.3 %all_gather.37 = bf16[16,32,256]{2,1,0:T(8,128)(2,1)S(1)} all-gather(bf16[1,32,256]{2,1,0:T(8,128)(2,1)S(1)} %get-tuple-element.6), channel_id=1, replica_groups=mesh['row'=16,'col'=16] {'col'}, dimensions={0}, use_global_device_ids=true | all-gather | bytes 278528 | tf_op jit(solution)/shard_map/all_gather | solution.py:33
  679.0 6.3 fusion.41
  690.8 50.2 %all_gather.36 = bf16[16,32,256]{2,1,0:T(8,128)(2,1)S(1)} all-gather(bf16[1,32,256]{2,1,0:T(8,128)(2,1)S(1)} %get-tuple-element.6), channel_id=1, replica_groups=mesh['row'=16,'col'=16] {'row'}, dimensions={0}, use_global_device_ids=true | all-gather | bytes 278528 | tf_op jit(solution)/shard_map/all_gather | solution.py:32
  742.9 7.6 fusion.38
  756.0 26.2 %reduce-scatter.25.cloned.1.call-done = f32[1,32,256]{2,1,0:T(8,128)} async-done(((f32[16,32,256]{2,1,0:T(8,128)}), f32[1,32,256]{2,1,0:T(8,128)}) %reduce-scatter.25.cloned.1.call-update) | async-done | bytes 32784 | tf_op jit(solution)/shard_map/reduce_scatter | solution.py:55
  782.2 74.2 %reduce-scatter.23.cloned.1.call-done = f32[1,32,256]{2,1,0:T(8,128)} async-done(((f32[16,32,256]{2,1,0:T(8,128)}), f32[1,32,256]{2,1,0:T(8,128)}) %reduce-scatter.23.cloned.1.call-update) | async-done | bytes 32784 | tf_op jit(solution)/shard_map/reduce_scatter | solution.py:54
  857.2 33.1 %all_gather.39 = bf16[16,32,256]{2,1,0:T(8,128)(2,1)S(1)} all-gather(bf16[1,32,256]{2,1,0:T(8,128)(2,1)S(1)} %fusion.99), channel_id=1, replica_groups=mesh['row'=16,'col'=16] {'col'}, dimensions={0}, use_global_device_ids=true | all-gather | bytes 278528 | tf_op jit(solution)/shard_map/all_gather | solution.py:33
  892.1 6.3 fusion.47
  903.9 50.8 %all_gather.38 = bf16[16,32,256]{2,1,0:T(8,128)(2,1)S(1)} all-gather(bf16[1,32,256]{2,1,0:T(8,128)(2,1)S(1)} %fusion.99), channel_id=1, replica_groups=mesh['row'=16,'col'=16] {'row'}, dimensions={0}, use_global_device_ids=true | all-gather | bytes 278528 | tf_op jit(solution)/shard_map/all_gather | solution.py:32
  956.6 7.6 fusion.44
  969.6 26.2 %reduce-scatter.29.cloned.1.call-done = f32[1,32,256]{2,1,0:T(8,128)} async-done(((f32[16,32,256]{2,1,0:T(8,128)}), f32[1,32,256]{2,1,0:T(8,128)}) %reduce-scatter.29.cloned.1.call-update) | async-done | bytes 32784 | tf_op jit(solution)/shard_map/reduce_scatter | solution.py:55
  995.8 74.1 %reduce-scatter.27.cloned.1.call-done = f32[1,32,256]{2,1,0:T(8,128)} async-done(((f32[16,32,256]{2,1,0:T(8,128)}), f32[1,32,256]{2,1,0:T(8,128)}) %reduce-scatter.27.cloned.1.call-update) | async-done | bytes 32784 | tf_op jit(solution)/shard_map/reduce_scatter | solution.py:54
  (85 shorter events, 70.3 us)
Async XLA Ops:
  6.5 135.5 %reduce-scatter.13.cloned.1.call-start = ((), (), s32[]{:S(2)}) async-start(), calls=%async_computation.11 | async-start | bytes 557056 | tf_op jit(solution)/shard_map/reduce_scatter | solution.py:55
  60.8 0.8 copy-start.2
  61.7 154.8 %reduce-scatter.11.cloned.1.call-start = ((), (), s32[]{:S(2)}) async-start(), calls=%async_computation.10 | async-start | bytes 557056 | tf_op jit(solution)/shard_map/reduce_scatter | solution.py:54
  110.7 105.7 %copy-start.10 = (f32[32,1,1,1,256]{4,3,2,1,0:T(1,128)S(1)}, f32[32,1,1,1,256]{4,3,2,1,0:T(1,128)}, u32[]{:S(2)}) copy-start(f32[32,1,1,1,256]{4,3,2,1,0:T(1,128)} %param.5) | copy-start | bytes 98308
  115.3 0.8 copy-start.3
  116.1 239.4 %reduce-scatter.17.cloned.1.call-start = ((), (), s32[]{:S(2)}) async-start(), calls=%async_computation.13 | async-start | bytes 557056 | tf_op jit(solution)/shard_map/reduce_scatter | solution.py:55
  263.1 0.8 copy-start.4
  264.0 165.0 %reduce-scatter.15.cloned.1.call-start = ((), (), s32[]{:S(2)}) async-start(), calls=%async_computation.12 | async-start | bytes 557056 | tf_op jit(solution)/shard_map/reduce_scatter | solution.py:54
  328.6 0.8 copy-start.5
  329.5 239.4 %reduce-scatter.21.cloned.1.call-start = ((), (), s32[]{:S(2)}) async-start(), calls=%async_computation.15 | async-start | bytes 557056 | tf_op jit(solution)/shard_map/reduce_scatter | solution.py:55
  476.5 0.8 copy-start.6
  477.3 165.7 %reduce-scatter.19.cloned.1.call-start = ((), (), s32[]{:S(2)}) async-start(), calls=%async_computation.14 | async-start | bytes 557056 | tf_op jit(solution)/shard_map/reduce_scatter | solution.py:54
  541.9 0.8 copy-start.7
  542.7 239.5 %reduce-scatter.25.cloned.1.call-start = ((), (), s32[]{:S(2)}) async-start(), calls=%async_computation.17 | async-start | bytes 557056 | tf_op jit(solution)/shard_map/reduce_scatter | solution.py:55
  689.9 0.8 copy-start.8
  690.8 165.6 %reduce-scatter.23.cloned.1.call-start = ((), (), s32[]{:S(2)}) async-start(), calls=%async_computation.16 | async-start | bytes 557056 | tf_op jit(solution)/shard_map/reduce_scatter | solution.py:54
  755.1 0.8 copy-start.9
  755.9 239.9 %reduce-scatter.29.cloned.1.call-start = ((), (), s32[]{:S(2)}) async-start(), calls=%async_computation.19 | async-start | bytes 557056 | tf_op jit(solution)/shard_map/reduce_scatter | solution.py:55
  903.0 0.8 copy-start.1
  903.9 166.0 %reduce-scatter.27.cloned.1.call-start = ((), (), s32[]{:S(2)}) async-start(), calls=%async_computation.18 | async-start | bytes 557056 | tf_op jit(solution)/shard_map/reduce_scatter | solution.py:54
  964.3 105.6 %copy-start.11 = (f32[1,32,256]{2,1,0:T(8,128)S(1)}, f32[1,32,256]{2,1,0:T(8,128)}, u32[]{:S(2)}) copy-start(f32[1,32,256]{2,1,0:T(8,128)} %reduce-scatter.25.cloned.1.call-done) | copy-start | bytes 98308
  964.3 105.6 %copy-start.12 = (f32[1,32,256]{2,1,0:T(8,128)S(1)}, f32[1,32,256]{2,1,0:T(8,128)}, u32[]{:S(2)}) copy-start(f32[1,32,256]{2,1,0:T(8,128)} %reduce-scatter.23.cloned.1.call-done) | copy-start | bytes 98308
  968.8 0.8 copy-start
Sparse Core Ops, SparseCore 0:
  61.8 80.2 reduce-scatter.12
  144.7 71.6 reduce-scatter.10
  264.1 91.2 reduce-scatter.16
  357.9 71.0 reduce-scatter.14
  477.4 91.4 reduce-scatter.20
  571.4 71.6 reduce-scatter.18
  690.9 91.2 reduce-scatter.24
  784.8 71.5 reduce-scatter.22
  904.0 91.7 reduce-scatter.28
  998.3 71.5 reduce-scatter.26
where the time goes:
time: 1090 us; the launch traced here: 1080 us
  waiting for transfers between devices  501 us (46%)
  blocking collectives  414 us (38%)
  matrix products  69.8 us (6%)
  other arithmetic  50.8 us (5%)
  local copies, waits for them, and re-layouts  28.1 us (3%)
  between operations  13.9 us (1%)
    reduce_scatter x5, waiting for transfers between devices, per_device(): lax.psum_scatter(forward_part, 'col', scatter_dimension=0, tiled=True)  370 us
    all_gather x5, blocking collectives, per_device(): col_pieces = lax.all_gather(rounded, 'row', axis=0, tiled=True)  242 us
    all_gather x5, blocking collectives, per_device(): row_pieces = lax.all_gather(rounded, 'col', axis=0, tiled=True)  173 us
    reduce_scatter x5, waiting for transfers between devices, per_device(): lax.psum_scatter(mirror_part, 'row', scatter_dimension=0, tiled=True)  130 us
    dot_general x5, matrix products, per_device(): jnp.einsum('svb,sab->sva', col_inputs, tile_set, preferred_element_type=j...  38.1 us
    dot_general x5, matrix products, per_device(): jnp.einsum('sva,sab->svb', row_inputs, tile_set, preferred_element_type=j...  31.7 us
    scatter-add x5, other arithmetic, per_device(): mirror_part = jnp.zeros((rows_count * blk_count, vec_count, tile_width),...  22.6 us
    scatter-add x5, other arithmetic, per_device(): forward_part = jnp.zeros((cols_count * blk_count, vec_count, tile_width),...  22.6 us
  transfers between devices with their start and end apart: 10, of which 10 were waited for; matrix products, arithmetic and copies ran while one was open for 6% of the time, Pallas kernels for 0%

commit v1 on v0

v1 whole, which is shorter than its diff:
```python
import functools

import jax
import jax.numpy as jnp
from jax import lax
from jax.experimental import pallas as pl
from jax.experimental.pallas import tpu as pltpu
from jax.sharding import PartitionSpec as P

MESH = pl.DeviceIdType.MESH
DEG = 5
CENTER = 0.5
HALF_WIDTH = 3.0
GROUP = 16
SLOTS = 80
VEC = 32
BS = 256
HB = 128
LOADS = 8

COL_STEPS = [(dx, dz) for dx in range(4) for dz in range(4) if dx or dz]
PAIR_STEPS = [(dy, dk) for dy in range(4) for dk in range(2) if dy or dk]


def kernel(
    meta, vec, tiles_hbm, out,
    tiles, flipped, run_m, run_f, now, before,
    yc_0, yc_1, yr, rows, send_m, recv_m, send_z, recv_z, send_f, recv_f,
    load_sem,
    yc_send, yc_recv, yr_send, yr_recv, yz_send, yz_recv, yf_send, yf_recv,
    m_send, m_recv, z_send, z_recv, f_send, f_recv,
):
    row, col = lax.axis_index("row"), lax.axis_index("col")
    half = row // 8
    pair = row % 8
    yc = (yc_0, yc_1)
    y, core = pair // 2, pair % 2
    x, z = col // 4, col % 4
    other = (1 - half) * 8

    col_ids = [((x + dx) % 4) * 4 + (z + dz) % 4 for dx, dz in COL_STEPS]
    pair_ids = [((y + dy) % 4) * 2 + (core + dk) % 2 for dy, dk in PAIR_STEPS]
    far = other + pair

    def remote(src, dst, send, recv, to):
        return pltpu.make_async_remote_copy(
            src_ref=src, dst_ref=dst, send_sem=send, recv_sem=recv,
            device_id=to, device_id_type=MESH,
        )

    def take(ref, sem):
        pltpu.make_async_copy(ref, ref, sem).wait()

    def load(n):
        rows = pl.ds(n * (SLOTS // LOADS), SLOTS // LOADS)
        return pltpu.make_async_copy(tiles_hbm.at[rows], tiles.at[rows], load_sem.at[n])

    for n in range(LOADS):
        load(n).start()

    barrier = pltpu.get_barrier_semaphore()
    for c in col_ids:
        pl.semaphore_signal(barrier, inc=1, device_id=(row, c), device_id_type=MESH)
    for p in pair_ids:
        pl.semaphore_signal(barrier, inc=1, device_id=(half * 8 + p, col), device_id_type=MESH)
    pl.semaphore_signal(barrier, inc=1, device_id=(far, col), device_id_type=MESH)

    now[...] = vec[...]
    before[...] = vec[...]
    run_m[0, SLOTS] = jnp.zeros((VEC, BS), jnp.float32)
    run_m[1, SLOTS] = jnp.zeros((VEC, BS), jnp.float32)
    run_f[0, SLOTS] = jnp.zeros((VEC, HB), jnp.float32)
    run_f[1, SLOTS] = jnp.zeros((VEC, HB), jnp.float32)

    def place(par, h):
        block = now[:, h * HB : (h + 1) * HB].astype(jnp.bfloat16)
        yc[h][col] = block
        yr[par, row, h] = block

    def spread_col(h):
        for c in col_ids:
            remote(yc[h].at[col], yc[h].at[col], yc_send.at[h], yc_recv.at[h], (row, c)).start()

    def spread_row(par):
        mine = yr.at[par, row]
        remote(mine, mine, yz_send.at[par], yz_recv.at[par], (far, col)).start()
        for p in pair_ids:
            remote(mine, mine, yr_send.at[par], yr_recv.at[par], (half * 8 + p, col)).start()

    place(0, 0)
    place(0, 1)
    pl.semaphore_wait(barrier, len(col_ids) + len(pair_ids) + 1)
    spread_col(0)
    spread_col(1)
    spread_row(0)

    for n in range(LOADS):
        load(n).wait()

        def flip(s, carry):
            flipped[s] = tiles[s].T
            return carry

        lax.fori_loop(n * (SLOTS // LOADS), (n + 1) * (SLOTS // LOADS), flip, 0, unroll=True)

    def mirror(h):
        total = None
        for p in range(SLOTS):
            s, b = meta[0, p], meta[1, p]
            term = jnp.dot(
                yc[h][b], tiles[s, h * HB : (h + 1) * HB, :], preferred_element_type=jnp.float32
            )
            total = term if p == 0 else jnp.where(meta[2, p] == 1, term, total + term)
            run_m[h, p] = total

    def forward(h):
        total = None
        for p in range(SLOTS):
            s, b = meta[4, p], meta[5, p]
            term = jnp.dot(
                rows[b], flipped[s, :, h * HB : (h + 1) * HB], preferred_element_type=jnp.float32
            )
            total = term if p == 0 else jnp.where(meta[6, p] == 1, term, total + term)
            run_f[h, p] = total

    def mirror_block(r):
        last = meta[3, r]
        return (run_m[0, last] + run_m[1, last]).astype(jnp.bfloat16)

    def step(t, carry):
        par = lax.rem(t, 2)

        take(yr.at[par, 0], yz_recv.at[par])
        theirs = yr.at[par, far]
        for p in pair_ids:
            remote(theirs, theirs, yf_send.at[par], yf_recv.at[par], (half * 8 + p, col)).start()

        take(yc[0].at[pl.ds(0, 15)], yc_recv.at[0])
        mirror(0)
        take(yc[1].at[pl.ds(0, 15)], yc_recv.at[1])
        mirror(1)

        for q, base in ((0, other), (1, half * 8)):
            block = mirror_block(base + pair)
            recv_m[par, q, pair, 0] = block[:, :HB]
            recv_m[par, q, pair, 1] = block[:, HB:]
            for n, p in enumerate(pair_ids):
                block = mirror_block(base + p)
                send_m[q, n, 0] = block[:, :HB]
                send_m[q, n, 1] = block[:, HB:]
                remote(
                    send_m.at[q, n], recv_m.at[par, q, pair], m_send.at[q], m_recv.at[par, q],
                    (half * 8 + p, col),
                ).start()

        take(yr.at[par, pl.ds(0, 7)], yr_recv.at[par])
        take(yr.at[par, pl.ds(0, 7)], yf_recv.at[par])
        for r in range(GROUP):
            rows[r, :, :HB] = yr[par, r, 0]
            rows[r, :, HB:] = yr[par, r, 1]
        for h in range(2):
            forward(h)
            recv_f[h, col] = run_f[h, meta[7, col]].astype(jnp.bfloat16)
            for n, c in enumerate(col_ids):
                send_f[h, n] = run_f[h, meta[7, c]].astype(jnp.bfloat16)
                remote(
                    send_f.at[h, n], recv_f.at[h, col], f_send.at[h], f_recv.at[h], (row, c)
                ).start()

        take(recv_m.at[par, 0, pl.ds(0, 7)], m_recv.at[par, 0])
        for h in range(2):
            part = recv_m[par, 0, 0, h].astype(jnp.float32)
            for n in range(1, 8):
                part = part + recv_m[par, 0, n, h].astype(jnp.float32)
            send_z[h] = part.astype(jnp.bfloat16)
        remote(send_z, recv_z.at[par], z_send, z_recv.at[par], (far, col)).start()

        take(recv_m.at[par, 1, pl.ds(0, 7)], m_recv.at[par, 1])
        take(yr.at[par, 0], yz_send.at[par])
        take(yr.at[par, pl.ds(0, 7)], yr_send.at[par])
        take(yr.at[par, pl.ds(0, 7)], yf_send.at[par])
        take(recv_z.at[par], z_recv.at[par])
        scale = jnp.where(t == 0, 1.0, 2.0).astype(jnp.float32)
        keep = jnp.where(t == 0, 0.0, 1.0).astype(jnp.float32)
        for h in range(2):
            cut = slice(h * HB, (h + 1) * HB)
            take(recv_f.at[h, pl.ds(0, 15)], f_recv.at[h])
            take(yc[h].at[pl.ds(0, 15)], yc_send.at[h])
            total = recv_z[par, h].astype(jnp.float32)
            for n in range(8):
                total = total + recv_m[par, 1, n, h].astype(jnp.float32)
            for n in range(GROUP):
                total = total + recv_f[h, n].astype(jnp.float32)
            present = now[:, cut]
            scaled = (total - CENTER * present) * (1.0 / HALF_WIDTH)
            following = scale * scaled - keep * before[:, cut]
            before[:, cut] = present
            now[:, cut] = following

            @pl.when(t < DEG - 1)
            def _():
                place(1 - par, h)
                spread_col(h)

        @pl.when(t < DEG - 1)
        def _():
            spread_row(1 - par)

        for h in range(2):
            take(send_f.at[h], f_send.at[h])
            take(send_m.at[h], m_send.at[h])
        take(send_z, z_send)
        return carry

    lax.fori_loop(0, DEG, step, 0)
    out[...] = now[...]


def ordered(key, block):
    slots = jnp.arange(SLOTS, dtype=jnp.int32)
    ahead = (key[None, :] < key[:, None]) | (
        (key[None, :] == key[:, None]) & (slots[None, :] < slots[:, None])
    )
    rank = jnp.sum(ahead, axis=1, dtype=jnp.int32)
    chosen = rank[None, :] == slots[:, None]
    slot = jnp.sum(jnp.where(chosen, slots[None, :], 0), axis=1, dtype=jnp.int32)
    source = jnp.sum(jnp.where(chosen, block[None, :], 0), axis=1, dtype=jnp.int32)
    group = jnp.sum(jnp.where(chosen, key[None, :], 0), axis=1, dtype=jnp.int32)
    start = jnp.concatenate([jnp.ones((1,), jnp.int32), (group[1:] != group[:-1]).astype(jnp.int32)])
    classes = jnp.arange(GROUP, dtype=jnp.int32)[:, None]
    upto = jnp.sum(key[None, :] <= classes, axis=1, dtype=jnp.int32)
    some = jnp.any(key[None, :] == classes, axis=1)
    last = jnp.where(some, upto - 1, SLOTS)
    pad = lambda a: jnp.pad(a, (0, 128 - a.shape[0]))
    return [pad(slot), pad(source), pad(start), pad(last)]


def per_device(vectors, tiles, pattern):
    slot_pairs = pattern[0, 0]
    live = slot_pairs[:, 0] >= 0
    row_key = jnp.where(live, slot_pairs[:, 0] % GROUP, GROUP)
    col_key = jnp.where(live, slot_pairs[:, 1] // GROUP, GROUP)
    row_block = jnp.where(live, row_key, 0)
    col_block = jnp.where(live, col_key, 0)
    meta = jnp.stack(ordered(col_key, row_block) + ordered(row_key, col_block))

    half16 = (VEC, HB)
    dma = pltpu.SemaphoreType.DMA
    filtered = pl.pallas_call(
        kernel,
        out_shape=jax.ShapeDtypeStruct((VEC, BS), jnp.float32),
        in_specs=[
            pl.BlockSpec(memory_space=pltpu.SMEM),
            pl.BlockSpec(memory_space=pltpu.VMEM),
            pl.BlockSpec(memory_space=pl.ANY),
        ],
        out_specs=pl.BlockSpec(memory_space=pltpu.VMEM),
        scratch_shapes=[
            pltpu.VMEM((SLOTS, BS, BS), jnp.bfloat16),
            pltpu.VMEM((SLOTS, BS, BS), jnp.bfloat16),
            pltpu.VMEM((2, SLOTS + 1, VEC, BS), jnp.float32),
            pltpu.VMEM((2, SLOTS + 1, VEC, HB), jnp.float32),
            pltpu.VMEM((VEC, BS), jnp.float32),
            pltpu.VMEM((VEC, BS), jnp.float32),
            pltpu.VMEM((GROUP,) + half16, jnp.bfloat16),
            pltpu.VMEM((GROUP,) + half16, jnp.bfloat16),
            pltpu.VMEM((2, GROUP, 2) + half16, jnp.bfloat16),
            pltpu.VMEM((GROUP, VEC, BS), jnp.bfloat16),
            pltpu.VMEM((2, 7, 2) + half16, jnp.bfloat16),
            pltpu.VMEM((2, 2, 8, 2) + half16, jnp.bfloat16),
            pltpu.VMEM((2,) + half16, jnp.bfloat16),
            pltpu.VMEM((2, 2) + half16, jnp.bfloat16),
            pltpu.VMEM((2, 15) + half16, jnp.bfloat16),
            pltpu.VMEM((2, GROUP) + half16, jnp.bfloat16),
            dma((LOADS,)),
            dma((2,)), dma((2,)), dma((2,)), dma((2,)), dma((2,)), dma((2,)), dma((2,)), dma((2,)),
            dma((2,)), dma((2, 2)), dma, dma((2,)), dma((2,)), dma((2,)),
        ],
        compiler_params=pltpu.CompilerParams(
            collective_id=0, has_side_effects=True, vmem_limit_bytes=48 * 2**20
        ),
        cost_estimate=pl.CostEstimate(
            flops=DEG * 4 * SLOTS * VEC * BS * BS, bytes_accessed=SLOTS * BS * BS * 2, transcendentals=0
        ),
        name="chebyshev",
    )(meta, vectors.reshape(VEC, BS), tiles.reshape(SLOTS, BS, BS))
    return filtered.reshape(VEC, 1, 1, 1, BS)


def solution(mesh):
    placed = (
        P(None, None, "row", "col", None),
        P("row", "col", None, None, None),
        P("row", "col", None, None),
    )
    return jax.shard_map(
        per_device,
        mesh=mesh,
        in_specs=placed,
        out_specs=P(None, None, "row", "col", None),
        check_vma=False,
    )
```

time: 1090 us -> 128 us (0.12); the launches traced: 1080 us -> 128 us
  waiting for transfers between devices: 501 us -> 0 us
  blocking collectives: 414 us -> 0 us
  Pallas kernels: 0 us -> 124 us
  matrix products: 69.8 us -> 0 us
  other arithmetic: 50.8 us -> 2.65 us
  local copies, waits for them, and re-layouts: 28.1 us -> 1.46 us
  between operations: 13.9 us -> 0.08 us
    reduce_scatter x10 -> x0, waiting for transfers between devices: 501 us -> none  [the longest x5 370 us: per_device(): lax.psum_scatter(forward_part, 'col', scatter_dimension=0, tiled=True)]
    all_gather x10 -> x0, blocking collectives: 414 us -> none  [the longest x5 242 us: per_device(): col_pieces = lax.all_gather(rounded, 'row', axis=0, tiled=True)]
    pallas_call x0 -> x1, Pallas kernels: none -> 124 us  [per_device(): pl.pallas_call(kernel, out_shape=jax.ShapeDtypeStruct((VEC, BS), jnp.floa...]
    dot_general x10 -> x0, matrix products: 69.8 us -> none  [the longest x5 38.1 us: per_device(): jnp.einsum('svb,sab->sva', col_inputs, tile_set, preferred_element_type=j...]
    scatter-add x10 -> x0, other arithmetic: 45.2 us -> none  [the longest x5 22.6 us: per_device(): mirror_part = jnp.zeros((rows_count * blk_count, vec_count, tile_width),...]
    gather x10 -> x0, local copies, waits for them, and re-layouts: 18.2 us -> none  [the longest x5 9.09 us: per_device(): col_inputs = jnp.take(col_pieces, mirror_index, axis=0)]
  transfers between devices with their start and end apart: 10 -> 0, of which waited for: 10 -> 0; matrix products, arithmetic and copies ran while one was open for 6% -> 0% of each run, Pallas kernels for 0% -> 0%
where the time goes in v1:
time: 128 us
  Pallas kernels  124 us (97%)
  other arithmetic  2.65 us (2%)
  local copies, waits for them, and re-layouts  1.46 us (1%)
    pallas_call x1, Pallas kernels, per_device(): pl.pallas_call(kernel, out_shape=jax.ShapeDtypeStruct((VEC, BS), jnp.floa...  124 us

profile of v1, /device:TPU:1, one launch (start us, length us, event | category | flops | bytes accessed | tf_op | source)
XLA Modules:
  0.0 127.8 jit_solution(10253922667068077028)
XLA Ops:
  0.0 0.8 fusion.12
  0.8 0.8 broadcast_select_fusion
  1.5 0.2 convert_reduce_fusion
  1.7 0.2 convert_reduce_fusion.1
  1.9 0.2 select_reduce_fusion
  2.1 0.1 slice_compare_fusion
  2.2 0.1 pad_add_fusion
  2.3 0.1 slice_compare_fusion.1
  2.4 0.1 pad_add_fusion.1
  2.5 0.1 fusion.4
  2.6 0.1 convert_reduce_fusion.2
  2.8 0.8 copy.8
  3.5 123.6 %chebyshev.1 = f32[32,256]{1,0:T(8,128)S(1)} custom-call(s32[8,128]{1,0:T(8,128)S(1)} %stack.43.meta, f32[32,256]{1,0:T(8,128)S(1)} %bitcast.51, bf16[80,256,256]{2,1,0:T(8,128)(2,1)} %bitcast.54), custom_call_target="tpu_custom_call" | custom-call | flops 3355443200 | bytes 10485760 | tf_op jit(solution)/shard_map/chebyshev/pallas_call | solution.py:249
  127.1 0.6 copy.5
  (11 shorter events, 0.1 us)

commit v2 on v1

v2 whole, which is shorter than its diff:
```python
import functools

import jax
import jax.numpy as jnp
from jax import lax
from jax.experimental import pallas as pl
from jax.experimental.pallas import tpu as pltpu
from jax.sharding import PartitionSpec as P

MESH = pl.DeviceIdType.MESH
DEG = 5
CENTER = 0.5
HALF_WIDTH = 3.0
GROUP = 16
SLOTS = 80
VEC = 32
BS = 256
HB = 128
LOADS = 8

PAIR_STEPS = [(dy, dk) for dy in (2, 1, 3, 0) for dk in range(2) if dy or dk]


def kernel(
    vec, pattern, tiles_hbm, out,
    tiles, flipped, run_m, run_f, now, before, table, meta,
    yc, yr, rows, send_m, recv_m, send_z, recv_z, send_x, recv_x, send_w, recv_w, gathered,
    load_sem, meta_sem,
    cz_send, cz_recv, cx_send, cx_recv, yr_send, yr_recv, yz_send, yz_recv, yf_send, yf_recv,
    m_send, m_recv, z_send, z_recv, x_send, x_recv, w_send, w_recv,
):
    row, col = lax.axis_index("row"), lax.axis_index("col")
    half = row // 8
    pair = row % 8
    y, core = pair // 2, pair % 2
    x, z = col // 4, col % 4
    other = (1 - half) * 8
    far = other + pair

    z_near = [z + 1 - 2 * (z % 2), (z + 2) % 4, 3 - z]
    x_near = [(x + 2) % 4, (x + 1) % 4, (x + 3) % 4]
    pair_ids = [((y + dy) % 4) * 2 + (core + dk) % 2 for dy, dk in PAIR_STEPS]

    def remote(src, dst, send, recv, to):
        return pltpu.make_async_remote_copy(
            src_ref=src, dst_ref=dst, send_sem=send, recv_sem=recv,
            device_id=to, device_id_type=MESH,
        )

    def take(ref, sem):
        pltpu.make_async_copy(ref, ref, sem).wait()

    def load(n):
        part = pl.ds(n * (SLOTS // LOADS), SLOTS // LOADS)
        return pltpu.make_async_copy(tiles_hbm.at[part], tiles.at[part], load_sem.at[n])

    barrier = pltpu.get_barrier_semaphore()
    greeted = [(far, col)]
    greeted += [(row, x * 4 + b) for b in z_near]
    greeted += [(row, a * 4 + z) for a in x_near]
    greeted += [(half * 8 + p, col) for p in pair_ids]
    for to in greeted:
        pl.semaphore_signal(barrier, inc=1, device_id=to, device_id_type=MESH)

    for n in range(LOADS):
        load(n).start()

    for h in range(2):
        block = vec[pl.ds(h, VEC, stride=2), :]
        now[h] = block
        before[h] = block
        run_m[h, SLOTS] = jnp.zeros((VEC, BS), jnp.float32)
        run_f[h, SLOTS] = jnp.zeros((VEC, HB), jnp.float32)

    def place(par):
        block = jnp.concatenate([now[0], now[1]], axis=1).astype(jnp.bfloat16)
        yc[col] = block
        yr[par, row] = block

    def spread(par):
        mine = yr.at[par, row]
        remote(mine, mine, yz_send.at[par], yz_recv.at[par], (far, col)).start()
        mine = yc.at[col]
        for n, b in enumerate(z_near):
            remote(mine, mine, cz_send, cz_recv.at[n], (row, x * 4 + b)).start()
        for a in x_near:
            remote(mine, mine, cx_send, cx_recv, (row, a * 4 + z)).start()
        mine = yr.at[par, row]
        for p in pair_ids:
            remote(mine, mine, yr_send.at[par], yr_recv.at[par], (half * 8 + p, col)).start()

    place(0)
    pl.semaphore_wait(barrier, len(greeted))
    spread(0)

    table[...] = jnp.full((8, 128), -1, jnp.int32)
    table[0:2, 0:SLOTS] = pattern[...]
    ids = table[...]
    live = ids >= 0
    keys = jnp.where(live, jnp.concatenate([ids[0:1] % GROUP, ids[1:2] // GROUP, ids[2:8]], axis=0), GROUP)
    down = lax.broadcasted_iota(jnp.int32, (128, 128), 0)
    along = lax.broadcasted_iota(jnp.int32, (128, 128), 1)

    def across(line):
        return jnp.broadcast_to(line, (128, 128))

    row_across, col_across = across(keys[0:1]), across(keys[1:2])
    row_down, col_down = row_across.T, col_across.T

    def count(mask, value=1):
        return jnp.sum(jnp.where(mask, value, 0), axis=0, keepdims=True)

    lines = []
    for key, key_down, source_down in (
        (col_across, col_down, row_down), (row_across, row_down, col_down)
    ):
        rank = count((key_down < key) | ((key_down == key) & (down < along)))
        chosen = across(rank).T == along
        group = count(chosen, key_down)
        lines.append(count(chosen, down))
        lines.append(count(chosen & (source_down < GROUP), source_down))
        lines.append((group != pltpu.roll(group, 1, 1)).astype(jnp.int32))
        lines.append(jnp.where(count(key_down == along) > 0, count(key_down <= along) - 1, SLOTS))
    for n, line in enumerate(lines):
        table[n : n + 1, :] = line
    tell = pltpu.make_async_copy(table, meta, meta_sem)
    tell.start()

    def flip_all():
        for n in range(LOADS):
            load(n).wait()

            def flip(s, carry):
                flipped[s] = tiles[s].T
                return carry

            lax.fori_loop(n * (SLOTS // LOADS), (n + 1) * (SLOTS // LOADS), flip, 0, unroll=True)
        tell.wait()

    def mirror(h):
        total = None
        for p in range(SLOTS):
            s, b = meta[0, p], meta[1, p]
            cut = slice(h * HB, (h + 1) * HB)
            term = jnp.dot(yc[b, :, cut], tiles[s, cut, :], preferred_element_type=jnp.float32)
            total = term if p == 0 else jnp.where(meta[2, p] == 1, term, total + term)
            run_m[h, p] = total

    def forward(h):
        total = None
        for p in range(SLOTS):
            s, b = meta[4, p], meta[5, p]
            cut = slice(h * HB, (h + 1) * HB)
            term = jnp.dot(rows[b], flipped[s, :, cut], preferred_element_type=jnp.float32)
            total = term if p == 0 else jnp.where(meta[6, p] == 1, term, total + term)
            run_f[h, p] = total

    def mirror_block(r):
        last = meta[3, r]
        return (run_m[0, last] + run_m[1, last]).astype(jnp.bfloat16)

    def forward_block(h, c):
        return run_f[h, meta[7, c]].astype(jnp.bfloat16)

    def step(t, carry):
        par = lax.rem(t, 2)

        for n, b in enumerate(z_near):
            theirs = yc.at[x * 4 + b]
            take(theirs, cz_recv.at[n])
            for a in x_near:
                remote(theirs, theirs, cx_send, cx_recv, (row, a * 4 + z)).start()
        theirs = yr.at[par, far]
        take(theirs, yz_recv.at[par])
        for p in pair_ids:
            remote(theirs, theirs, yf_send.at[par], yf_recv.at[par], (half * 8 + p, col)).start()

        @pl.when(t == 0)
        def _():
            flip_all()

        take(yc.at[pl.ds(0, 12)], cx_recv)
        mirror(0)
        mirror(1)

        for q, base in ((0, other), (1, half * 8)):
            for n, p in enumerate(pair_ids):
                send_m[q, n] = mirror_block(base + p)
                remote(
                    send_m.at[q, n], recv_m.at[par, q, pair], m_send.at[q], m_recv.at[par, q],
                    (half * 8 + p, col),
                ).start()
            recv_m[par, q, pair] = mirror_block(base + pair)

        take(yc.at[pl.ds(0, 12)], cx_send)
        take(yc.at[pl.ds(0, 3)], cz_send)
        take(yr.at[par, pl.ds(0, 7)], yr_recv.at[par])
        take(yr.at[par, pl.ds(0, 7)], yf_recv.at[par])
        for r in range(GROUP):
            rows[r] = yr[par, r]
        for h in range(2):
            forward(h)
            for n, a in enumerate(x_near):
                for b in range(4):
                    send_x[h, n, b] = forward_block(h, a * 4 + b)
                remote(
                    send_x.at[h, n], recv_x.at[h, x], x_send.at[h], x_recv.at[h], (row, a * 4 + z)
                ).start()
            for b in range(4):
                recv_x[h, x, b] = forward_block(h, x * 4 + b)

        take(recv_m.at[par, 0, pl.ds(0, 7)], m_recv.at[par, 0])
        part = recv_m[par, 0, 0].astype(jnp.float32)
        for n in range(1, 8):
            part = part + recv_m[par, 0, n].astype(jnp.float32)
        send_z[...] = part.astype(jnp.bfloat16)
        remote(send_z, recv_z.at[par], z_send, z_recv.at[par], (far, col)).start()

        for h in range(2):
            take(recv_x.at[h, pl.ds(0, 3)], x_recv.at[h])
            for n, b in enumerate(z_near + [z]):
                part = recv_x[h, 0, b].astype(jnp.float32)
                for a in range(1, 4):
                    part = part + recv_x[h, a, b].astype(jnp.float32)
                if n < 3:
                    send_w[h, n] = part.astype(jnp.bfloat16)
                    remote(
                        send_w.at[h, n], recv_w.at[h, z], w_send.at[h], w_recv.at[h], (row, x * 4 + b)
                    ).start()
                else:
                    recv_w[h, z] = part.astype(jnp.bfloat16)

        take(recv_m.at[par, 1, pl.ds(0, 7)], m_recv.at[par, 1])
        part = recv_m[par, 1, 0].astype(jnp.float32)
        for n in range(1, 8):
            part = part + recv_m[par, 1, n].astype(jnp.float32)
        gathered[...] = part

        take(yr.at[par, 0], yz_send.at[par])
        take(yr.at[par, pl.ds(0, 7)], yr_send.at[par])
        take(yr.at[par, pl.ds(0, 7)], yf_send.at[par])
        take(recv_z.at[par], z_recv.at[par])
        gathered[...] += recv_z[par].astype(jnp.float32)
        scale = jnp.where(t == 0, 1.0, 2.0).astype(jnp.float32)
        keep = jnp.where(t == 0, 0.0, 1.0).astype(jnp.float32)
        for h in range(2):
            take(recv_w.at[h, pl.ds(0, 3)], w_recv.at[h])
            total = gathered[:, h * HB : (h + 1) * HB]
            for b in range(4):
                total = total + recv_w[h, b].astype(jnp.float32)
            present = now[h]
            scaled = (total - CENTER * present) * (1.0 / HALF_WIDTH)
            following = scale * scaled - keep * before[h]
            before[h] = present
            now[h] = following

        @pl.when(t < DEG - 1)
        def _():
            place(1 - par)
            spread(1 - par)

        for h in range(2):
            take(send_x.at[h], x_send.at[h])
            take(send_w.at[h], w_send.at[h])
            take(send_m.at[h], m_send.at[h])
        take(send_z, z_send)
        return carry

    lax.fori_loop(0, DEG, step, 0)
    for h in range(2):
        out[pl.ds(h, VEC, stride=2), :] = now[h]


def per_device(vectors, tiles, pattern):
    bf16, f32 = jnp.bfloat16, jnp.float32
    dma = pltpu.SemaphoreType.DMA
    vmem = pltpu.VMEM
    filtered = pl.pallas_call(
        kernel,
        out_shape=jax.ShapeDtypeStruct((VEC * 2, HB), f32),
        in_specs=[
            pl.BlockSpec(memory_space=pltpu.VMEM),
            pl.BlockSpec(memory_space=pltpu.VMEM),
            pl.BlockSpec(memory_space=pl.ANY),
        ],
        out_specs=pl.BlockSpec(memory_space=pltpu.VMEM),
        scratch_shapes=[
            vmem((SLOTS, BS, BS), bf16),
            vmem((SLOTS, BS, BS), bf16),
            vmem((2, SLOTS + 1, VEC, BS), f32),
            vmem((2, SLOTS + 1, VEC, HB), f32),
            vmem((2, VEC, HB), f32),
            vmem((2, VEC, HB), f32),
            vmem((8, 128), jnp.int32),
            pltpu.SMEM((8, 128), jnp.int32),
            vmem((GROUP, VEC, BS), bf16),
            vmem((2, GROUP, VEC, BS), bf16),
            vmem((GROUP, VEC, BS), bf16),
            vmem((2, 7, VEC, BS), bf16),
            vmem((2, 2, 8, VEC, BS), bf16),
            vmem((VEC, BS), bf16),
            vmem((2, VEC, BS), bf16),
            vmem((2, 3, 4, VEC, HB), bf16),
            vmem((2, 4, 4, VEC, HB), bf16),
            vmem((2, 3, VEC, HB), bf16),
            vmem((2, 4, VEC, HB), bf16),
            vmem((VEC, BS), f32),
            dma((LOADS,)), dma,
            dma, dma((3,)), dma, dma, dma((2,)), dma((2,)), dma((2,)), dma((2,)), dma((2,)), dma((2,)),
            dma((2,)), dma((2, 2)), dma, dma((2,)), dma((2,)), dma((2,)), dma((2,)), dma((2,)),
        ],
        compiler_params=pltpu.CompilerParams(
            collective_id=0, has_side_effects=True, vmem_limit_bytes=48 * 2**20
        ),
        cost_estimate=pl.CostEstimate(
            flops=DEG * 4 * SLOTS * VEC * BS * BS, bytes_accessed=SLOTS * BS * BS * 2, transcendentals=0
        ),
        name="chebyshev",
    )(vectors.reshape(VEC * 2, HB), pattern[0, 0].T, tiles.reshape(SLOTS, BS, BS))
    return filtered.reshape(VEC, 1, 1, 1, BS)


def solution(mesh):
    placed = (
        P(None, None, "row", "col", None),
        P("row", "col", None, None, None),
        P("row", "col", None, None),
    )
    return jax.shard_map(
        per_device,
        mesh=mesh,
        in_specs=placed,
        out_specs=P(None, None, "row", "col", None),
        check_vma=False,
    )
```

time: 128 us -> 107 us (0.84)
  Pallas kernels: 124 us -> 104 us
  other arithmetic: 2.65 us -> 0 us
    pallas_call x1, Pallas kernels: 124 us -> 104 us  [per_device(): pl.pallas_call(kernel, out_shape=jax.ShapeDtypeStruct((VEC * 2, HB), f32)...]
    unnamed x1 -> x5, local copies, waits for them, and re-layouts: 0.76 us -> 2.05 us
where the time goes in v2:
time: 107 us; the launch traced here: 106 us
  Pallas kernels  104 us (97%)
  local copies, waits for them, and re-layouts  2.05 us (2%)
    pallas_call x1, Pallas kernels, per_device(): pl.pallas_call(kernel, out_shape=jax.ShapeDtypeStruct((VEC * 2, HB), f32)...  104 us

profile of v2, /device:TPU:1, one launch (start us, length us, event | category | flops | bytes accessed | tf_op | source)
XLA Modules:
  0.0 105.9 jit_solution(14335441625009233306)
XLA Ops:
  0.0 0.0 copy-start
  0.0 0.8 copy-done
  0.8 0.0 copy-start.1
  0.8 0.7 copy-done.1
  1.4 103.8 %chebyshev.1 = f32[64,128]{1,0:T(8,128)S(1)} custom-call(f32[64,128]{1,0:T(8,128)S(1)} %bitcast.7, s32[2,80]{1,0:T(2,128)S(1)} %bitcast.8, bf16[80,256,256]{2,1,0:T(8,128)(2,1)} %bitcast.9), custom_call_target="tpu_custom_call" | custom-call | flops 3355443200 | bytes 10485760 | tf_op jit(solution)/shard_map/chebyshev/pallas_call | solution.py:278
  105.3 0.6 copy.6
Async XLA Ops:
  0.0 0.8 copy-start
  0.8 0.7 copy-start.1

commit v3 on v2

v3 whole, which is shorter than its diff:
```python
import functools

import jax
import jax.numpy as jnp
from jax import lax
from jax.experimental import pallas as pl
from jax.experimental.pallas import tpu as pltpu
from jax.sharding import PartitionSpec as P

MESH = pl.DeviceIdType.MESH
DEG = 5
CENTER = 0.5
HALF_WIDTH = 3.0
GROUP = 16
SLOTS = 80
VEC = 32
BS = 256
HB = 128
LOADS = 8

PAIR_STEPS = [(dy, dk) for dy in (2, 1, 3, 0) for dk in range(2) if dy or dk]


def kernel(
    vec_hbm, pattern_hbm, tiles_hbm, out,
    vec, pattern,
    tiles, flipped, run_m, run_f, now, before, table, meta,
    yc_0, yc_1, yr, rows, send_m, recv_m, send_z, recv_z, send_x, recv_x, send_w, recv_w, recv_d, recv_e, gathered,
    load_sem, meta_sem, in_sem,
    cz_send, cz_recv, cx_send, cx_recv, yr_send, yr_recv, yz_send, yz_recv, yf_send, yf_recv,
    m_send, m_recv, z_send, z_recv, x_send, x_recv, w_send, w_recv, d_recv, e_recv,
):
    row, col = lax.axis_index("row"), lax.axis_index("col")
    yc = (yc_0, yc_1)
    half = row // 8
    pair = row % 8
    y, core = pair // 2, pair % 2
    x, z = col // 4, col % 4
    other = (1 - half) * 8
    far = other + pair

    z_near = [3 - z, (z + 2) % 4, z + 1 - 2 * (z % 2)]
    edge, inner = z % 3 == 0, z % 3 != 0
    upper, lower = half == 0, half == 1
    x_near = [(x + 2) % 4, (x + 1) % 4, (x + 3) % 4]
    pair_ids = [((y + dy) % 4) * 2 + (core + dk) % 2 for dy, dk in PAIR_STEPS]

    def remote(src, dst, send, recv, to):
        return pltpu.make_async_remote_copy(
            src_ref=src, dst_ref=dst, send_sem=send, recv_sem=recv,
            device_id=to, device_id_type=MESH,
        )

    def take(ref, sem):
        pltpu.make_async_copy(ref, ref, sem).wait()

    def load(n):
        part = pl.ds(n * (SLOTS // LOADS), SLOTS // LOADS)
        return pltpu.make_async_copy(tiles_hbm.at[part], tiles.at[part], load_sem.at[n])

    vec_in = pltpu.make_async_copy(vec_hbm, vec, in_sem.at[0])
    pattern_in = pltpu.make_async_copy(pattern_hbm, pattern, in_sem.at[1])
    vec_in.start()
    pattern_in.start()

    barrier = pltpu.get_barrier_semaphore()
    greeted = [(far, col)]
    greeted += [(row, x * 4 + b) for b in z_near]
    greeted += [(row, a * 4 + z) for a in x_near]
    greeted += [(row, x_near[0] * 4 + z_near[1])]
    greeted += [(row, a * 4 + z_near[0]) for a in x_near]
    greeted += [(half * 8 + p, col) for p in pair_ids]
    for to in greeted:
        pl.semaphore_signal(barrier, inc=1, device_id=to, device_id_type=MESH)

    for n in range(LOADS):
        load(n).start()

    vec_in.wait()
    for h in range(2):
        block = vec[pl.ds(h, VEC, stride=2), :]
        now[h] = block
        before[h] = block
        run_m[h, SLOTS] = jnp.zeros((VEC, BS), jnp.float32)
        run_f[h, SLOTS] = jnp.zeros((VEC, HB), jnp.float32)

    def place(par, h):
        block = now[h].astype(jnp.bfloat16)
        yc[h][col] = block
        yr[par, h, row] = block

    def spread(par, h):
        @pl.when(lower)
        def _():
            mine = yr.at[par, h, row]
            remote(mine, mine, yz_send.at[par, h], yz_recv.at[par, h], (far, col)).start()

        mine = yc[h].at[col]
        for n, b in enumerate(z_near):
            remote(mine, mine, cz_send.at[h], cz_recv.at[h, n], (row, x * 4 + b)).start()

        @pl.when(edge)
        def _():
            for a in x_near:
                remote(
                    mine, mine, cx_send.at[h], cx_recv.at[h], (row, a * 4 + z_near[0])
                ).start()

        remote(
            mine, mine, cx_send.at[h], cx_recv.at[h], (row, x_near[0] * 4 + z_near[1])
        ).start()
        for a in x_near:
            remote(mine, mine, cx_send.at[h], cx_recv.at[h], (row, a * 4 + z)).start()
        row_block = yr.at[par, h, row]
        for p in pair_ids:
            remote(
                row_block, row_block, yr_send.at[par, h], yr_recv.at[par, h], (half * 8 + p, col)
            ).start()

    @pl.when(lower)
    def _():
        for r in range(8):
            for par in range(2):
                for h in range(2):
                    yr[par, h, r] = jnp.zeros((VEC, HB), jnp.bfloat16)

    place(0, 0)
    place(0, 1)
    pl.semaphore_wait(barrier, len(greeted))
    spread(0, 0)
    spread(0, 1)

    pattern_in.wait()
    table[...] = jnp.full((8, 128), -1, jnp.int32)
    table[0:2, 0:SLOTS] = pattern[...]
    ids = table[...]
    live = ids >= 0
    keys = jnp.where(live, jnp.concatenate([ids[0:1] % GROUP, ids[1:2] // GROUP, ids[2:8]], axis=0), GROUP)
    down = lax.broadcasted_iota(jnp.int32, (128, 128), 0)
    along = lax.broadcasted_iota(jnp.int32, (128, 128), 1)

    def across(line):
        return jnp.broadcast_to(line, (128, 128))

    row_across, col_across = across(keys[0:1]), across(keys[1:2])
    row_down, col_down = row_across.T, col_across.T

    def count(mask, value=1):
        return jnp.sum(jnp.where(mask, value, 0), axis=0, keepdims=True)

    lines = []
    for key, key_down, source_down in (
        (col_across, col_down, row_down), (row_across, row_down, col_down)
    ):
        rank = count((key_down < key) | ((key_down == key) & (down < along)))
        chosen = across(rank).T == along
        group = count(chosen, key_down)
        lines.append(count(chosen, down))
        lines.append(count(chosen & (source_down < GROUP), source_down))
        lines.append((group != pltpu.roll(group, 1, 1)).astype(jnp.int32))
        lines.append(jnp.where(count(key_down == along) > 0, count(key_down <= along) - 1, SLOTS))
    for n, line in enumerate(lines):
        table[n : n + 1, :] = line
    tell = pltpu.make_async_copy(table, meta, meta_sem)
    tell.start()

    def flip_all():
        for n in range(LOADS):
            load(n).wait()

            def flip(s, carry):
                flipped[s] = tiles[s].T
                return carry

            lax.fori_loop(n * (SLOTS // LOADS), (n + 1) * (SLOTS // LOADS), flip, 0, unroll=True)
        tell.wait()

    def mirror(h):
        total = None
        for p in range(SLOTS):
            s, b = meta[0, p], meta[1, p]
            cut = slice(h * HB, (h + 1) * HB)
            term = jnp.dot(yc[h][b], tiles[s, cut, :], preferred_element_type=jnp.float32)
            total = term if p == 0 else jnp.where(meta[2, p] == 1, term, total + term)
            run_m[h, p] = total

    def forward(h):
        total = None
        for p in range(SLOTS):
            s, b = meta[4, p], meta[5, p]
            cut = slice(h * HB, (h + 1) * HB)
            term = jnp.dot(rows[b], flipped[s, :, cut], preferred_element_type=jnp.float32)
            total = term if p == 0 else jnp.where(meta[6, p] == 1, term, total + term)
            run_f[h, p] = total

    def mirror_block(r):
        last = meta[3, r]
        return (run_m[0, last] + run_m[1, last]).astype(jnp.bfloat16)

    def forward_block(h, c):
        return run_f[h, meta[7, c]].astype(jnp.bfloat16)

    def step(t, carry):
        par = lax.rem(t, 2)

        def pass_on(h, n, near):
            theirs = yc[h].at[x * 4 + z_near[n]]
            take(theirs, cz_recv.at[h, n])
            for a in near:
                remote(theirs, theirs, cx_send.at[h], cx_recv.at[h], (row, a * 4 + z)).start()

        for h in range(2):
            pass_on(h, 2, x_near)

            @pl.when(inner)
            def _():
                pass_on(h, 0, x_near)

            pass_on(h, 1, x_near[1:])

        @pl.when(upper)
        def _():
            for h in range(2):
                theirs = yr.at[par, h, far]
                take(theirs, yz_recv.at[par, h])
                for p in pair_ids:
                    remote(
                        theirs, theirs, yf_send.at[par, h], yf_recv.at[par, h],
                        (half * 8 + p, col),
                    ).start()

        @pl.when(t == 0)
        def _():
            flip_all()

        @pl.when(edge)
        def _():
            for h in range(2):
                pass_on(h, 0, [])

        for h in range(2):
            take(yc[h].at[pl.ds(0, 12)], cx_recv.at[h])
            mirror(h)

        def hand_out(q, base):
            for n, p in enumerate(pair_ids + [pair]):
                block = mirror_block(base + p)
                for h in range(2):
                    piece = block[:, h * HB : (h + 1) * HB]
                    if n < 7:
                        send_m[h, q, n] = piece
                    else:
                        recv_m[par, h, q, pair] = piece
            for h in range(2):
                for n, p in enumerate(pair_ids):
                    remote(
                        send_m.at[h, q, n], recv_m.at[par, h, q, pair],
                        m_send.at[h, q], m_recv.at[par, h, q], (half * 8 + p, col),
                    ).start()

        @pl.when(upper)
        def _():
            hand_out(0, other)

        hand_out(1, half * 8)

        for h in range(2):
            take(yc[h].at[pl.ds(0, 12)], cx_send.at[h])
            take(yc[h].at[pl.ds(0, 3)], cz_send.at[h])
        for h in range(2):
            take(yr.at[par, h, pl.ds(0, 7)], yr_recv.at[par, h])

            @pl.when(upper)
            def _():
                take(yr.at[par, h, pl.ds(0, 7)], yf_recv.at[par, h])

            for r in range(GROUP):
                rows[r, :, h * HB : (h + 1) * HB] = yr[par, h, r]
        for h in range(2):
            forward(h)

            def to_line(n, b, near):
                for m, a in near:
                    send_x[h, n, m] = forward_block(h, a * 4 + b)
                    remote(
                        send_x.at[h, n, m], recv_x.at[h, n, x], x_send.at[h], x_recv.at[h, n],
                        (row, a * 4 + z),
                    ).start()
                recv_x[h, n, x] = forward_block(h, x * 4 + b)

            def to_owner(n, m, dst, sem):
                a, b = x_near[m], z_near[n]
                send_x[h, n, m] = forward_block(h, a * 4 + b)
                remote(
                    send_x.at[h, n, m], dst, x_send.at[h], sem, (row, a * 4 + b)
                ).start()

            numbered = list(enumerate(x_near))

            @pl.when(edge)
            def _():
                for m in range(3):
                    to_owner(0, m, recv_e.at[h, x], e_recv.at[h])
                send_w[h, 0] = forward_block(h, x * 4 + z_near[0])
                remote(
                    send_w.at[h, 0], recv_w.at[h, z], w_send.at[h], w_recv.at[h],
                    (row, x * 4 + z_near[0]),
                ).start()

            to_line(1, z_near[1], numbered[1:])

            @pl.when(inner)
            def _():
                to_line(0, z_near[0], numbered)

            to_line(2, z_near[2], numbered)
            to_owner(1, 0, recv_d.at[h], d_recv.at[h])
            to_line(3, z, numbered)

        def summed(ref, places):
            total = ref[places[0]].astype(jnp.float32)
            for n in places[1:]:
                total = total + ref[n].astype(jnp.float32)
            return total

        @pl.when(upper)
        def _():
            for h in range(2):
                take(recv_m.at[par, h, 0, pl.ds(0, 7)], m_recv.at[par, h, 0])
                send_z[h] = summed(recv_m.at[par, h, 0], range(8)).astype(jnp.bfloat16)
                remote(
                    send_z.at[h], recv_z.at[par, h], z_send.at[h], z_recv.at[par, h], (far, col)
                ).start()

        def line_sum(h, n, places):
            take(recv_x.at[h, n, pl.ds(0, len(places) - 1)], x_recv.at[h, n])
            part = summed(recv_x.at[h, n], places).astype(jnp.bfloat16)
            if n < 3:
                send_w[h, n] = part
                remote(
                    send_w.at[h, n], recv_w.at[h, z], w_send.at[h], w_recv.at[h],
                    (row, x * 4 + z_near[n]),
                ).start()
            else:
                recv_w[h, z] = part

        for h in range(2):
            line_sum(h, 1, [x] + x_near[1:])

            @pl.when(inner)
            def _():
                line_sum(h, 0, range(4))

            line_sum(h, 2, range(4))
            line_sum(h, 3, range(4))
            take(recv_m.at[par, h, 1, pl.ds(0, 7)], m_recv.at[par, h, 1])
            gathered[h] = summed(recv_m.at[par, h, 1], range(8))

        scale = jnp.where(t == 0, 1.0, 2.0).astype(jnp.float32)
        keep = jnp.where(t == 0, 0.0, 1.0).astype(jnp.float32)
        for h in range(2):
            take(recv_d.at[h], d_recv.at[h])
            gathered[h] += recv_d[h].astype(jnp.float32)

            @pl.when(edge)
            def _():
                take(recv_e.at[h, pl.ds(0, 3)], e_recv.at[h])
                gathered[h] += summed(recv_e.at[h], x_near)

            @pl.when(lower)
            def _():
                take(recv_z.at[par, h], z_recv.at[par, h])
                gathered[h] += recv_z[par, h].astype(jnp.float32)

            take(recv_w.at[h, pl.ds(0, 3)], w_recv.at[h])
            total = gathered[h] + summed(recv_w.at[h], range(4))
            present = now[h]
            scaled = (total - CENTER * present) * (1.0 / HALF_WIDTH)
            following = scale * scaled - keep * before[h]
            before[h] = present
            now[h] = following

            @pl.when(t < DEG - 1)
            def _():
                place(1 - par, h)
                spread(1 - par, h)

        for h in range(2):
            take(yr.at[par, h, pl.ds(0, 7)], yr_send.at[par, h])
            take(send_m.at[h, 1], m_send.at[h, 1])
            take(send_x.at[h], x_send.at[h])
            take(send_w.at[h], w_send.at[h])

        @pl.when(upper)
        def _():
            for h in range(2):
                take(yr.at[par, h, pl.ds(0, 7)], yf_send.at[par, h])
                take(send_m.at[h, 0], m_send.at[h, 0])
                take(send_z.at[h], z_send.at[h])

        @pl.when(lower)
        def _():
            for h in range(2):
                take(yr.at[par, h, 0], yz_send.at[par, h])

        return carry

    lax.fori_loop(0, DEG, step, 0)
    for h in range(2):
        out[pl.ds(h, VEC, stride=2), :] = now[h]


def per_device(vectors, tiles, pattern):
    bf16, f32 = jnp.bfloat16, jnp.float32
    dma = pltpu.SemaphoreType.DMA
    vmem = pltpu.VMEM
    filtered = pl.pallas_call(
        kernel,
        out_shape=jax.ShapeDtypeStruct((VEC * 2, HB), f32),
        in_specs=[
            pl.BlockSpec(memory_space=pltpu.HBM),
            pl.BlockSpec(memory_space=pltpu.HBM),
            pl.BlockSpec(memory_space=pltpu.HBM),
        ],
        out_specs=pl.BlockSpec(memory_space=pltpu.VMEM),
        scratch_shapes=[
            vmem((VEC * 2, HB), f32),
            vmem((2, SLOTS), jnp.int32),
            vmem((SLOTS, BS, BS), bf16),
            vmem((SLOTS, BS, BS), bf16),
            vmem((2, SLOTS + 1, VEC, BS), f32),
            vmem((2, SLOTS + 1, VEC, HB), f32),
            vmem((2, VEC, HB), f32),
            vmem((2, VEC, HB), f32),
            vmem((8, 128), jnp.int32),
            pltpu.SMEM((8, 128), jnp.int32),
            vmem((GROUP, VEC, HB), bf16),
            vmem((GROUP, VEC, HB), bf16),
            vmem((2, 2, GROUP, VEC, HB), bf16),
            vmem((GROUP, VEC, BS), bf16),
            vmem((2, 2, 7, VEC, HB), bf16),
            vmem((2, 2, 2, 8, VEC, HB), bf16),
            vmem((2, VEC, HB), bf16),
            vmem((2, 2, VEC, HB), bf16),
            vmem((2, 4, 3, VEC, HB), bf16),
            vmem((2, 4, 4, VEC, HB), bf16),
            vmem((2, 3, VEC, HB), bf16),
            vmem((2, 4, VEC, HB), bf16),
            vmem((2, VEC, HB), bf16),
            vmem((2, 4, VEC, HB), bf16),
            vmem((2, VEC, HB), f32),
            dma((LOADS,)), dma, dma((2,)),
            dma((2,)), dma((2, 3)), dma((2,)), dma((2,)),
            dma((2, 2)), dma((2, 2)), dma((2, 2)), dma((2, 2)), dma((2, 2)), dma((2, 2)),
            dma((2, 2)), dma((2, 2, 2)), dma((2,)), dma((2, 2)),
            dma((2,)), dma((2, 4)), dma((2,)), dma((2,)), dma((2,)), dma((2,)),
        ],
        compiler_params=pltpu.CompilerParams(
            collective_id=0, has_side_effects=True, vmem_limit_bytes=48 * 2**20
        ),
        cost_estimate=pl.CostEstimate(
            flops=DEG * 4 * SLOTS * VEC * BS * BS, bytes_accessed=SLOTS * BS * BS * 2, transcendentals=0
        ),
        name="chebyshev",
    )(vectors.reshape(VEC * 2, HB), pattern[0, 0].T, tiles.reshape(SLOTS, BS, BS))
    return filtered.reshape(VEC, 1, 1, 1, BS)


def solution(mesh):
    placed = (
        P(None, None, "row", "col", None),
        P("row", "col", None, None, None),
        P("row", "col", None, None),
    )
    return jax.shard_map(
        per_device,
        mesh=mesh,
        in_specs=placed,
        out_specs=P(None, None, "row", "col", None),
        check_vma=False,
    )
```

time: 107 us -> 101 us (0.944)
  Pallas kernels: 104 us -> 98.5 us
    pallas_call x1, Pallas kernels: 104 us -> 98.5 us  [per_device(): pl.pallas_call(kernel, out_shape=jax.ShapeDtypeStruct((VEC * 2, HB), f32)...]
where the time goes in v3:
time: 101 us
  Pallas kernels  98.5 us (98%)
  local copies, waits for them, and re-layouts  2.05 us (2%)
    pallas_call x1, Pallas kernels, per_device(): pl.pallas_call(kernel, out_shape=jax.ShapeDtypeStruct((VEC * 2, HB), f32)...  98.5 us
    unnamed x5, local copies, waits for them, and re-layouts  2.05 us

profile of v3, /device:TPU:1, one launch (start us, length us, event | category | flops | bytes accessed | tf_op | source)
XLA Modules:
  0.0 100.6 jit_solution(13313519838308819655)
XLA Ops:
  0.0 0.0 copy-start
  0.0 0.8 copy-done
  0.8 0.0 copy-start.1
  0.8 0.7 copy-done.1
  1.4 98.5 %chebyshev.1 = f32[64,128]{1,0:T(8,128)S(1)} custom-call(f32[64,128]{1,0:T(8,128)S(1)} %bitcast.7, s32[2,80]{1,0:T(2,128)S(1)} %bitcast.8, bf16[80,256,256]{2,1,0:T(8,128)(2,1)} %bitcast.9), custom_call_target="tpu_custom_call" | custom-call | flops 3355443200 | bytes 10485760 | tf_op jit(solution)/shard_map/chebyshev/pallas_call | solution.py:417
  100.0 0.6 copy.6
Async XLA Ops:
  0.0 0.8 copy-start
  0.8 0.7 copy-start.1

commit v4 on v3

--- a/solution.py
+++ b/solution.py
@@ -126,9 +126,6 @@
 
     place(0, 0)
     place(0, 1)
-    pl.semaphore_wait(barrier, len(greeted))
-    spread(0, 0)
-    spread(0, 1)
 
     pattern_in.wait()
     table[...] = jnp.full((8, 128), -1, jnp.int32)
@@ -164,8 +161,8 @@
     tell = pltpu.make_async_copy(table, meta, meta_sem)
     tell.start()
 
-    def flip_all():
-        for n in range(LOADS):
+    def flip_part(parts):
+        for n in parts:
             load(n).wait()
 
             def flip(s, carry):
@@ -173,6 +170,14 @@
                 return carry
 
             lax.fori_loop(n * (SLOTS // LOADS), (n + 1) * (SLOTS // LOADS), flip, 0, unroll=True)
+
+    flip_part(range(2))
+    pl.semaphore_wait(barrier, len(greeted))
+    spread(0, 0)
+    spread(0, 1)
+
+    def flip_all():
+        flip_part(range(2, LOADS))
         tell.wait()
 
     def mirror(h):
@@ -353,6 +358,8 @@
 
             line_sum(h, 2, range(4))
             line_sum(h, 3, range(4))
+
+        for h in range(2):
             take(recv_m.at[par, h, 1, pl.ds(0, 7)], m_recv.at[par, h, 1])
             gathered[h] = summed(recv_m.at[par, h, 1], range(8))
 
@@ -456,7 +463,7 @@
             dma((2,)), dma((2, 4)), dma((2,)), dma((2,)), dma((2,)), dma((2,)),
         ],
         compiler_params=pltpu.CompilerParams(
-            collective_id=0, has_side_effects=True, vmem_limit_bytes=48 * 2**20
+            collective_id=0, has_side_effects=True, vmem_limit_bytes=63 * 2**20
         ),
         cost_estimate=pl.CostEstimate(
             flops=DEG * 4 * SLOTS * VEC * BS * BS, bytes_accessed=SLOTS * BS * BS * 2, transcendentals=0

time: 101 us -> 100 us (0.990)
    unnamed x5 -> x1, local copies, waits for them, and re-layouts: 2.05 us -> 1.38 us
where the time goes in v4:
time: 100 us; the launch traced here: 99.8 us
  Pallas kernels  98.4 us (98%)
  local copies, waits for them, and re-layouts  1.38 us (1%)
    pallas_call x1, Pallas kernels, per_device(): pl.pallas_call(kernel, out_shape=jax.ShapeDtypeStruct((VEC * 2, HB), f32)...  98.4 us

profile of v4, /device:TPU:1, one launch (start us, length us, event | category | flops | bytes accessed | tf_op | source)
XLA Modules:
  0.0 99.8 jit_solution(16032506659633483546)
XLA Ops:
  0.0 98.4 %chebyshev.1 = f32[64,128]{1,0:T(8,128)} custom-call(f32[64,128]{1,0:T(8,128)} %bitcast.8, s32[2,80]{1,0:T(2,128)} %bitcast.9, bf16[80,256,256]{2,1,0:T(8,128)(2,1)} %bitcast.7), custom_call_target="tpu_custom_call" | custom-call | flops 3355443200 | bytes 10485760 | tf_op jit(solution)/shard_map/chebyshev/pallas_call | solution.py:424
  98.4 1.4 %copy.6 = f32[32,1,1,1,256]{4,3,2,1,0:T(1,128)} copy(f32[32,1,1,1,256]{4,3,2,1,0:T(1,128)} %bitcast.6) | data formatting | bytes 65536
